TPU v7x, 128 devices: a whole 4x4x4 slice. The times are simulated.
128 devices in a mesh: inst: 4 (over x_hi, core), seq: 32 (over y, z, x_lo).
Axes of the slice: x: 4 (x_hi: 2, x_lo: 2; x = x_hi * 2 + x_lo), y: 4, z: 4, core: 2. Of those that a mesh axis runs over, the one named last changes fastest.
Arguments:
- query_rows: bfloat16 [16384, 8192], P(('inst', 'seq')), may hold values from -25 to 25
- key_rows: bfloat16 [16384, 1024], P(('inst', 'seq')), may hold values from -4 to 4
- value_rows: bfloat16 [16384, 1024], P(('inst', 'seq')), may hold values from -6 to 6
- target_instance: int32 [8192], P(('inst', 'seq')), may hold values from 0 to 3, as said below
- block_position: int32 [8192], P(('inst', 'seq')), may hold values from 0 to 2047, as said below
- request_lengths: int32 [4, 2], replicated, may hold values from 1 to 3584, 4096 in all within a row
Outputs:
- attended: bfloat16 [16384, 8192], P(('inst', 'seq'))
Inputs may be any that keep to these rules, and one draw needn't show every extreme that they name: `target_instance`: together with block_position, every pair of an instance and a position block is named by exactly one entry block. Of the 64 blocks of one entry device, at most 1 name one instance and block positions b (values of block_position) with the same b // 64, and at most 1 name one instance and block positions with the same min(h, 63 - h), where h = b // 32; both bounds are reached. `block_position`: see target_instance.
All inputs are finite; a program needn't handle non-finite values.
Results may differ from a plain program's by a relative error of at most 0.0055.
Values may be sent and summed in bfloat16 or wider, within the bound.
No kernel may reach another device: no remote copies, remote signals or barrier semaphores. Data moves between devices by JAX's collectives and lax.ppermute only.
A program may use at most 128 MiB of HBM per device.

v0:
```python
import math
import jax
import jax.numpy as jnp
from jax import lax
from jax.sharding import PartitionSpec as P

QUERY_HEADS = 64
KEY_HEADS = 8
HEAD_SIZE = 128


def layout_position(global_rows, row_count, block_rows, half_blocks):
    shard_of = global_rows // row_count
    local_rows = global_rows % row_count
    local_block = local_rows // block_rows
    within = local_rows % block_rows
    offset = local_block % half_blocks
    upper = local_block // half_blocks
    halves = 2 * shard_of + upper
    return (halves * half_blocks + offset) * block_rows + within


def shards(query_rows, key_rows, value_rows, target_instance, block_position, request_lengths):
    inst_count = lax.axis_size("inst")
    seq_count = lax.axis_size("seq")
    devices = inst_count * seq_count
    blocks = block_position.shape[0]
    row_count = query_rows.shape[0]
    block_rows = row_count // blocks
    half_blocks = blocks // 2
    capacity = blocks // (2 * seq_count)
    groups = QUERY_HEADS // KEY_HEADS
    query_width = query_rows.shape[1]
    key_width = key_rows.shape[1]
    score_scale = 1.0 / math.sqrt(HEAD_SIZE)
    own_shard = lax.axis_index("seq")
    instance = lax.axis_index("inst")
    halves = block_position // half_blocks
    offset = block_position % half_blocks
    owner_shard = halves // 2
    local_block = halves % 2 * half_blocks + offset
    target = target_instance * seq_count + owner_shard
    ordinal = jnp.arange(blocks)
    before = (target[:, None] == target[None, :]) & (ordinal[None, :] < ordinal[:, None])
    slot_index = jnp.sum(before.astype(jnp.int32), axis=1)
    destination = target * capacity + slot_index

    def pack_rows(payload, width):
        empty = jnp.zeros((devices * capacity, block_rows, width), payload.dtype)
        filled = empty.at[destination].set(payload.reshape(blocks, block_rows, width))
        return filled.reshape(inst_count, seq_count, capacity, block_rows, width)

    send_query = pack_rows(query_rows, query_width)
    send_key = pack_rows(key_rows, key_width)
    send_value = pack_rows(value_rows, key_width)
    labels = (
        jnp.full((devices * capacity,), -1.0, jnp.bfloat16)
        .at[destination]
        .set(local_block.astype(jnp.bfloat16))
    )
    labels = labels.reshape(inst_count, seq_count, capacity)
    got_query, got_key, got_value, got_label = (
        lax.all_to_all(
            send_query.reshape(devices, capacity, block_rows, query_width),
            ("inst", "seq"),
            split_axis=0,
            concat_axis=0,
            tiled=True,
        ),
        lax.all_to_all(
            send_key.reshape(devices, capacity, block_rows, key_width),
            ("inst", "seq"),
            split_axis=0,
            concat_axis=0,
            tiled=True,
        ),
        lax.all_to_all(
            send_value.reshape(devices, capacity, block_rows, key_width),
            ("inst", "seq"),
            split_axis=0,
            concat_axis=0,
            tiled=True,
        ),
        lax.all_to_all(
            labels.reshape(devices, capacity),
            ("inst", "seq"),
            split_axis=0,
            concat_axis=0,
            tiled=True,
        ),
    )
    received = got_label.reshape(-1).astype(jnp.int32)
    placed = jnp.where(received < 0, blocks, received)

    def unpack_rows(payload, width):
        empty = jnp.zeros((blocks, block_rows, width), payload.dtype)
        filled = empty.at[placed].set(payload.reshape(-1, block_rows, width), mode="drop")
        return filled.reshape(row_count, width)

    local_query = unpack_rows(got_query, query_width)
    local_key = unpack_rows(got_key, key_width)
    local_value = unpack_rows(got_value, key_width)
    lengths_here = lax.dynamic_index_in_dim(request_lengths, instance, 0, keepdims=False)
    request_ends = jnp.cumsum(lengths_here)
    query_pos = layout_position(
        own_shard * row_count + jnp.arange(row_count), row_count, block_rows, half_blocks
    )
    query_start = jnp.sum(
        jnp.where(request_ends[None, :] <= query_pos[:, None], lengths_here[None, :], 0), axis=1
    )
    query_heads = local_query.reshape(row_count, KEY_HEADS, groups, HEAD_SIZE)

    def attend(running, key_block, value_block, key_index):
        key_pos = layout_position(key_index, row_count, block_rows, half_blocks)
        allowed = (key_pos[None, :] <= query_pos[:, None]) & (
            key_pos[None, :] >= query_start[:, None]
        )
        maxima, totals, weighted = running
        key_heads = key_block.reshape(-1, KEY_HEADS, HEAD_SIZE)
        value_heads = value_block.reshape(-1, KEY_HEADS, HEAD_SIZE)
        scores = (
            jnp.einsum("qhgd,khd->hgqk", query_heads, key_heads, preferred_element_type=jnp.float32)
            * score_scale
        )
        masked = jnp.where(allowed, scores, -1e30)
        new_maxima = jnp.maximum(maxima, jnp.max(masked, axis=-1))
        weights = jnp.where(allowed, jnp.exp(scores - new_maxima[..., None]), 0.0)
        rescale = jnp.exp(maxima - new_maxima)
        totals = totals * rescale + jnp.sum(weights, axis=-1)
        weighted = weighted * rescale[..., None] + jnp.einsum(
            "hgqk,khd->hgqd",
            weights.astype(jnp.bfloat16),
            value_heads,
            preferred_element_type=jnp.float32,
        )
        return (new_maxima, totals, weighted)

    initial = (
        jnp.full((KEY_HEADS, groups, row_count), -1e30, jnp.float32),
        jnp.zeros((KEY_HEADS, groups, row_count), jnp.float32),
        jnp.zeros((KEY_HEADS, groups, row_count, HEAD_SIZE), jnp.float32),
    )
    running = initial
    key_piece = lax.all_gather(local_key, "seq", axis=0, tiled=True)
    value_piece = lax.all_gather(local_value, "seq", axis=0, tiled=True)
    piece_rows = key_piece.shape[0]
    shard_count = piece_rows // row_count
    keyed = key_piece.reshape(shard_count, row_count, key_width)
    valued = value_piece.reshape(shard_count, row_count, key_width)
    offsets = jnp.arange(shard_count) * row_count

    def scan_step(state, element):
        key_block, value_block, first_row = element
        return (attend(state, key_block, value_block, first_row + jnp.arange(row_count)), None)

    running, unused = lax.scan(scan_step, running, (keyed, valued, offsets))
    maxima, totals, weighted = running
    attended_local = (
        (weighted / totals[..., None])
        .transpose(2, 0, 1, 3)
        .reshape(row_count, query_width)
        .astype(jnp.bfloat16)
    )
    out_blocks = attended_local.reshape(blocks, block_rows, query_width)
    returning = out_blocks[jnp.clip(received, 0, blocks - 1)]
    returned = lax.all_to_all(
        returning.reshape(devices, capacity, block_rows, query_width),
        ("inst", "seq"),
        split_axis=0,
        concat_axis=0,
        tiled=True,
    )
    gathered_back = returned.reshape(devices * capacity, block_rows, query_width)[destination]
    return gathered_back.reshape(row_count, query_width)


def solution(mesh):
    placed = (
        P(("inst", "seq"), None),
        P(("inst", "seq"), None),
        P(("inst", "seq"), None),
        P(("inst", "seq")),
        P(("inst", "seq")),
        P(),
    )
    return jax.shard_map(
        shards, mesh=mesh, in_specs=placed, out_specs=P(("inst", "seq"), None), check_vma=False
    )
```

profile of v0, /device:TPU:1, one launch (start us, length us, event | category | flops | bytes accessed | tf_op | source)
XLA Modules:
  0.0 1056.4 jit_solution(14671933270696867781)
XLA Ops:
  9.8 11.5 %all-to-all-start = ((bf16[128,1,1]{2,1,0:T(2,128)(2,1)}), bf16[128,1,1]{2,1,0:T(2,128)(2,1)S(1)}, u32[]{:S(2)}, u32[]{:S(2)}) async-start(bf16[128,1,1]{2,1,0:T(2,128)(2,1)} %copy.43), calls=%async_computation | async-start | bytes 131072 | tf_op jit(solution)/shard_map/all_to_all | solution.py:84
  23.5 7.9 scatter_fusion.4
  31.4 9.8 all-to-all-start.3
  43.6 11.3 %all-to-all-done.3 = bf16[128,1,2,1024]{3,2,1,0:T(2,128)(2,1)S(1)} async-done(((bf16[128,1,2,1024]{3,2,1,0:T(2,128)(2,1)}), bf16[128,1,2,1024]{3,2,1,0:T(2,128)(2,1)S(1)}, u32[]{:S(2)}, u32[]{:S(2)}) %all-to-all-start.3) | async-done | bytes 524320 | tf_op jit(solution)/shard_map/all_to_all | solution.py:77
  55.0 4.5 scatter_fusion.5
  63.2 23.9 %all_to_all.29 = bf16[128,1,2,1024]{3,2,1,0:T(2,128)(2,1)S(1)} all-to-all(bf16[128,1,2,1024]{3,2,1,0:T(2,128)(2,1)S(1)} %bitcast.80), channel_id=1, replica_groups=mesh['inst'=4,'seq'=32] {'inst','seq'}, dimensions={0} | all-to-all | bytes 1048576 | tf_op jit(solution)/shard_map/all_to_all | solution.py:70
  87.3 4.5 scatter_fusion.1
  95.8 6.2 broadcast_in_dim.95
  101.9 14.6 %scatter_fusion.2 = bf16[128,2,8192]{2,1,0:T(2,128)(2,1)} fusion(bf16[128,2,8192]{2,1,0:T(2,128)(2,1)} %broadcast_in_dim.95, s32[64]{0:T(128)S(1)} %compare_select_fusion.21, bf16[64,2,8192]{2,1,0:T(2,128)(2,1)S(1)} %reshape.356), kind=kCustom, calls=%fused_computation.5 | custom fusion | bytes 6291712 | tf_op jit(solution)/shard_map/scatter | solution.py:50
  116.6 5.8 all-to-all-start.2
  122.9 99.8 %all-to-all-done.2 = bf16[128,1,2,8192]{3,2,1,0:T(2,128)(2,1)} async-done(((bf16[128,1,2,8192]{3,2,1,0:T(2,128)(2,1)}), bf16[128,1,2,8192]{3,2,1,0:T(2,128)(2,1)}, u32[]{:S(2)}, u32[]{:S(2)}) %all-to-all-start.2) | async-done | bytes 4194336 | tf_op jit(solution)/shard_map/all_to_all | solution.py:63
  224.7 20.7 %scatter_fusion.3 = bf16[64,2,8192]{2,1,0:T(2,128)(2,1)S(1)} fusion(bf16[64,2,8192]{2,1,0:T(2,128)(2,1)S(1)} %broadcast_in_dim.94, s32[128]{0:T(128)S(1)} %get-tuple-element.300, bf16[128,2,8192]{2,1,0:T(2,128)(2,1)} %bitcast.7), kind=kCustom, calls=%fused_computation.6 | custom fusion | bytes 12583424 | tf_op jit(solution)/shard_map/scatter | solution.py:97
  251.2 44.4 %all-gather.5.cloned.1.call-done = bf16[4096,1024]{1,0:T(8,128)(2,1)} async-done(((bf16[128,1024]{1,0:T(8,128)(2,1)}), bf16[4096,1024]{1,0:T(8,128)(2,1)}) %all-gather.5.cloned.1.call-update) | async-done | bytes 8388624 | tf_op jit(solution)/shard_map/all_gather | solution.py:145
  295.6 193.7 %all-gather.3.cloned.1.call-done = bf16[4096,1024]{1,0:T(8,128)(2,1)} async-done(((bf16[128,1024]{1,0:T(8,128)(2,1)}), bf16[4096,1024]{1,0:T(8,128)(2,1)}) %all-gather.3.cloned.1.call-update) | async-done | bytes 8388624 | tf_op jit(solution)/shard_map/all_gather | solution.py:144
  489.3 470.0 %while.18 = (s32[]{:T(128)}, f32[8,8,128]{2,1,0:T(8,128)S(1)}, f32[8,8,128]{2,1,0:T(8,128)S(1)}, f32[8,8,128,128]{3,2,1,0:T(8,128)}, s32[32]{0:T(128)S(1)}, /*in...) while((s32[]{:T(128)}, f32[8,8,128]{2,1,0:T(8,128)S(1)}, ...), condition=%wide.region_13.14_spmd.clone, body=%wide.region_10.13_spmd.clone.sunk | while | flops 551657472 | bytes 26282648 | solution.py:156
  494.7 3.2 fusion.50
  498.1 5.1 fusion.52
  508.6 3.2 fusion.50
  512.1 5.9 fusion.52
  523.4 3.2 fusion.50
  526.8 5.9 fusion.52
  541.5 5.9 fusion.52
  552.8 3.2 fusion.50
  556.2 5.9 fusion.52
  570.9 5.9 fusion.52
  582.2 3.2 fusion.50
  585.6 5.9 fusion.52
  596.9 3.2 fusion.50
  600.3 5.9 fusion.52
  615.0 5.9 fusion.52
  629.7 5.9 fusion.52
  644.5 5.9 fusion.52
  655.8 3.2 fusion.50
  659.2 5.9 fusion.52
  673.9 5.9 fusion.52
  688.6 5.9 fusion.52
  699.9 3.2 fusion.50
  703.3 5.9 fusion.52
  714.6 3.2 fusion.50
  718.0 5.9 fusion.52
  732.7 5.9 fusion.52
  747.4 5.9 fusion.52
  762.2 5.9 fusion.52
  776.9 5.9 fusion.52
  791.6 5.9 fusion.52
  802.9 3.2 fusion.50
  806.3 5.9 fusion.52
  817.6 3.2 fusion.50
  821.0 5.9 fusion.52
  835.7 5.9 fusion.52
  847.0 3.2 fusion.50
  850.4 5.9 fusion.52
  861.7 3.2 fusion.50
  865.1 5.9 fusion.52
  879.8 5.9 fusion.52
  894.6 5.9 fusion.52
  909.3 5.9 fusion.52
  924.0 5.9 fusion.52
  938.7 5.9 fusion.52
  953.4 5.9 fusion.52
  967.4 11.8 %gather_fusion = bf16[128,2,8192]{2,1,0:T(2,128)(2,1)} fusion(bf16[64,2,8192]{2,1,0:T(2,128)(2,1)S(1)} %convert_element_type.46, s32[1024]{0:T(1024)S(1)} %pad_clamp_fusion.1), kind=kCustom, calls=%fused_computation | custom fusion | bytes 8389120 | tf_op jit(solution)/shard_map/gather | solution.py:165
  979.1 6.6 all-to-all-start.4
  985.8 53.2 %all-to-all-done.4 = bf16[128,1,2,8192]{3,2,1,0:T(2,128)(2,1)} async-done(((bf16[128,1,2,8192]{3,2,1,0:T(2,128)(2,1)}), bf16[128,1,2,8192]{3,2,1,0:T(2,128)(2,1)}, u32[]{:S(2)}, u32[]{:S(2)}) %all-to-all-start.4) | async-done | bytes 4194336 | tf_op jit(solution)/shard_map/all_to_all | solution.py:166
  1038.9 8.4 gather_fusion.1
  (385 shorter events, 274.2 us)
Async XLA Ops:
  6.5 115.8 %copy-start = (s32[4,2]{0,1:T(2,128)S(1)}, s32[4,2]{0,1:T(2,128)}, u32[]{:S(2)}) copy-start(s32[4,2]{0,1:T(2,128)} %param.13) | copy-start | bytes 100
  6.5 53.9 %copy-start.2 = (bf16[128,1024]{1,0:T(8,128)(2,1)S(1)}, bf16[128,1024]{1,0:T(8,128)(2,1)}, u32[]{:S(2)}) copy-start(bf16[128,1024]{1,0:T(8,128)(2,1)} %param.9) | copy-start | bytes 786436
  9.8 21.5 %all-to-all-start = ((bf16[128,1,1]{2,1,0:T(2,128)(2,1)}), bf16[128,1,1]{2,1,0:T(2,128)(2,1)S(1)}, u32[]{:S(2)}, u32[]{:S(2)}) async-start(bf16[128,1,1]{2,1,0:T(2,128)(2,1)} %copy.43), calls=%async_computation | async-start | bytes 131072 | tf_op jit(solution)/shard_map/all_to_all | solution.py:84
  31.4 23.5 %all-to-all-start.3 = ((bf16[128,1,2,1024]{3,2,1,0:T(2,128)(2,1)}), bf16[128,1,2,1024]{3,2,1,0:T(2,128)(2,1)S(1)}, u32[]{:S(2)}, u32[]{:S(2)}) async-start(bf16[128,1,2,1024]{3,2,1,0:T(2,128)(2,1)} %bitcast.9), calls=%async_computation.3 | async-start | bytes 1048576 | tf_op jit(solution)/shard_map/all_to_all | solution.py:77
  41.1 254.4 %all-gather.5.cloned.1.call-start = ((), (), s32[]{:S(2)}) async-start(), calls=%async_computation.6 | async-start | bytes 8650752 | tf_op jit(solution)/shard_map/all_gather | solution.py:145
  60.3 428.9 %all-gather.3.cloned.1.call-start = ((), (), s32[]{:S(2)}) async-start(), calls=%async_computation.5 | async-start | bytes 8650752 | tf_op jit(solution)/shard_map/all_gather | solution.py:144
  116.6 106.1 %all-to-all-start.2 = ((bf16[128,1,2,8192]{3,2,1,0:T(2,128)(2,1)}), bf16[128,1,2,8192]{3,2,1,0:T(2,128)(2,1)}, u32[]{:S(2)}, u32[]{:S(2)}) async-start(bf16[128,1,2,8192]{3,2,1,0:T(2,128)(2,1)} %bitcast.78), calls=%async_computation.2 | async-start | bytes 8388608 | tf_op jit(solution)/shard_map/all_to_all | solution.py:63
  979.1 59.8 %all-to-all-start.4 = ((bf16[128,1,2,8192]{3,2,1,0:T(2,128)(2,1)}), bf16[128,1,2,8192]{3,2,1,0:T(2,128)(2,1)}, u32[]{:S(2)}, u32[]{:S(2)}) async-start(bf16[128,1,2,8192]{3,2,1,0:T(2,128)(2,1)} %bitcast.79), calls=%async_computation.4 | async-start | bytes 8388608 | tf_op jit(solution)/shard_map/all_to_all | solution.py:166
  1038.9 10.6 %copy-start.1 = (s32[4,2]{0,1:T(2,128)S(1)}, s32[4,2]{0,1:T(2,128)}, u32[]{:S(2)}) copy-start(s32[4,2]{0,1:T(2,128)} %param.13) | copy-start | bytes 100
Sparse Core Ops, SparseCore 0:
  60.5 235.0 all-gather.4
  297.2 192.0 all-gather.2
where the time goes:
time: 1060 us
  waiting for transfers between devices  402 us (38%)
  matrix products  277 us (26%)
  local copies, waits for them, and re-layouts  169 us (16%)
  other arithmetic  135 us (13%)
  starting transfers between devices  33.7 us (3%)
  blocking collectives  23.9 us (2%)
  between operations  13.6 us (1%)
    all_gather x1, waiting for transfers between devices, shards(): key_piece = lax.all_gather(local_key, 'seq', axis=0, tiled=True)  194 us
    dot_general x32, matrix products, attend(): jnp.einsum('hgqk,khd->hgqd', weights.astype(jnp.bfloat16), value_heads, p...  187 us
    reduce_sum x32, other arithmetic, attend(): totals = totals * rescale + jnp.sum(weights, axis=-1)  103 us
    all_to_all x1, waiting for transfers between devices, shards(): lax.all_to_all(send_query.reshape(devices, capacity, block_rows, query_wi...  99.8 us
    dot_general x32, matrix products, attend(): jnp.einsum('qhgd,khd->hgqk', query_heads, key_heads, preferred_element_ty...  90 us
    dynamic_slice x128, local copies, waits for them, and re-layouts, shards(): running, unused = lax.scan(scan_step, running, (keyed, valued, offsets))  63.7 us
    all_to_all x1, waiting for transfers between devices, shards(): lax.all_to_all(returning.reshape(devices, capacity, block_rows, query_wid...  53.2 us
    all_gather x1, waiting for transfers between devices, shards(): value_piece = lax.all_gather(local_value, 'seq', axis=0, tiled=True)  44.4 us
  transfers between devices with their start and end apart: 6, of which 5 were waited for; matrix products, arithmetic and copies ran while one was open for 7% of the time, Pallas kernels for 0%

commit v1 on v0

--- a/solution.py
+++ b/solution.py
@@ -141,7 +141,9 @@
         jnp.zeros((KEY_HEADS, groups, row_count, HEAD_SIZE), jnp.float32),
     )
     running = initial
-    key_piece = lax.all_gather(local_key, "seq", axis=0, tiled=True)
+    key_piece = jnp.concatenate(
+        lax.all_to_all(jnp.stack([local_key] * lax.axis_size("seq")), "seq", 0, 0), axis=0
+    )
     value_piece = lax.all_gather(local_value, "seq", axis=0, tiled=True)
     piece_rows = key_piece.shape[0]
     shard_count = piece_rows // row_count

time: 1060 us -> 1020 us (0.962)
  waiting for transfers between devices: 402 us -> 338 us
  local copies, waits for them, and re-layouts: 169 us -> 203 us
  blocking collectives: 23.9 us -> 0 us
  starting transfers between devices: 33.7 us -> 47.2 us
    all_gather x1 -> x0, waiting for transfers between devices: 194 us -> none  [shards(): key_piece = lax.all_gather(local_key, 'seq', axis=0, tiled=True)]
    all_to_all x0 -> x2, waiting for transfers between devices: none -> 178 us  [the longest x1 178 us: shards(): lax.all_to_all(jnp.stack([local_key] * lax.axis_size('seq')), 'seq', 0, 0)]
    all_gather x1, waiting for transfers between devices: 44.4 us -> 0.01 us  [shards(): value_piece = lax.all_gather(local_value, 'seq', axis=0, tiled=True)]
    all_to_all x1 -> x0, blocking collectives: 23.9 us -> none  [shards(): lax.all_to_all(send_key.reshape(devices, capacity, block_rows, key_width)...]
    dynamic_slice x128, local copies, waits for them, and re-layouts: 63.7 us -> 86.4 us  [shards(): running, unused = lax.scan(scan_step, running, (keyed, valued, offsets))]
  transfers between devices with their start and end apart: 6 -> 7, of which waited for: 5 -> 4; matrix products, arithmetic and copies ran while one was open for 7% -> 8% of each run, Pallas kernels for 0% -> 0%
where the time goes in v1:
time: 1020 us; the launch traced here: 1010 us
  waiting for transfers between devices  338 us (33%)
  matrix products  276 us (27%)
  local copies, waits for them, and re-layouts  203 us (20%)
  other arithmetic  135 us (13%)
  starting transfers between devices  47.2 us (5%)
  between operations  13.6 us (1%)
    dot_general x32, matrix products, attend(): jnp.einsum('hgqk,khd->hgqd', weights.astype(jnp.bfloat16), value_heads, p...  187 us
    all_to_all x1, waiting for transfers between devices, shards(): lax.all_to_all(jnp.stack([local_key] * lax.axis_size('seq')), 'seq', 0, 0)  178 us
    reduce_sum x32, other arithmetic, attend(): totals = totals * rescale + jnp.sum(weights, axis=-1)  103 us
    all_to_all x1, waiting for transfers between devices, shards(): lax.all_to_all(send_query.reshape(devices, capacity, block_rows, query_wi...  95.5 us
    dot_general x32, matrix products, attend(): jnp.einsum('qhgd,khd->hgqk', query_heads, key_heads, preferred_element_ty...  88.6 us
    dynamic_slice x128, local copies, waits for them, and re-layouts, shards(): running, unused = lax.scan(scan_step, running, (keyed, valued, offsets))  86.4 us
    all_to_all x1, waiting for transfers between devices, shards(): lax.all_to_all(returning.reshape(devices, capacity, block_rows, query_wid...  53.2 us
    scatter x3, local copies, waits for them, and re-layouts, pack_rows(): empty.at[destination].set(payload.reshape(blocks, block_rows, width))  30.5 us
  transfers between devices with their start and end apart: 7, of which 4 were waited for; matrix products, arithmetic and copies ran while one was open for 8% of the time, Pallas kernels for 0%

profile of v1, /device:TPU:1, one launch (start us, length us, event | category | flops | bytes accessed | tf_op | source)
XLA Modules:
  0.0 1013.0 jit_solution(8319132077649285125)
XLA Ops:
  9.8 11.5 %all-to-all-start = ((bf16[128,1,1]{2,1,0:T(2,128)(2,1)}), bf16[128,1,1]{2,1,0:T(2,128)(2,1)S(1)}, u32[]{:S(2)}, u32[]{:S(2)}) async-start(bf16[128,1,1]{2,1,0:T(2,128)(2,1)} %copy.45), calls=%async_computation | async-start | bytes 131072 | tf_op jit(solution)/shard_map/all_to_all | solution.py:84
  23.5 7.9 scatter_fusion.4
  31.4 9.8 all-to-all-start.4
  43.6 11.3 %all-to-all-done.4 = bf16[128,1,2,1024]{3,2,1,0:T(2,128)(2,1)S(1)} async-done(((bf16[128,1,2,1024]{3,2,1,0:T(2,128)(2,1)}), bf16[128,1,2,1024]{3,2,1,0:T(2,128)(2,1)S(1)}, u32[]{:S(2)}, u32[]{:S(2)}) %all-to-all-start.4) | async-done | bytes 524320 | tf_op jit(solution)/shard_map/all_to_all | solution.py:77
  55.0 4.5 scatter_fusion.5
  61.5 7.9 scatter_fusion
  69.4 4.5 all-to-all-start.1
  77.1 6.2 broadcast_in_dim.95
  83.3 14.6 %scatter_fusion.2 = bf16[128,2,8192]{2,1,0:T(2,128)(2,1)} fusion(bf16[128,2,8192]{2,1,0:T(2,128)(2,1)} %broadcast_in_dim.95, s32[64]{0:T(128)S(1)} %compare_select_fusion.21, bf16[64,2,8192]{2,1,0:T(2,128)(2,1)S(1)} %reshape.350), kind=kCustom, calls=%fused_computation.5 | custom fusion | bytes 6291712 | tf_op jit(solution)/shard_map/scatter | solution.py:50
  97.9 10.4 %all-to-all-start.3 = ((bf16[128,1,2,8192]{3,2,1,0:T(2,128)(2,1)}), bf16[128,1,2,8192]{3,2,1,0:T(2,128)(2,1)}, u32[]{:S(2)}, u32[]{:S(2)}) async-start(bf16[128,1,2,8192]{3,2,1,0:T(2,128)(2,1)} %bitcast.79), calls=%async_computation.3 | async-start | bytes 8388608 | tf_op jit(solution)/shard_map/all_to_all | solution.py:63
  108.5 4.5 scatter_fusion.1
  113.2 95.5 %all-to-all-done.3 = bf16[128,1,2,8192]{3,2,1,0:T(2,128)(2,1)} async-done(((bf16[128,1,2,8192]{3,2,1,0:T(2,128)(2,1)}), bf16[128,1,2,8192]{3,2,1,0:T(2,128)(2,1)}, u32[]{:S(2)}, u32[]{:S(2)}) %all-to-all-start.3) | async-done | bytes 4194336 | tf_op jit(solution)/shard_map/all_to_all | solution.py:63
  208.8 5.1 stack.3
  213.9 5.0 all-to-all-start.2
  221.4 20.7 %scatter_fusion.3 = bf16[64,2,8192]{2,1,0:T(2,128)(2,1)S(1)} fusion(bf16[64,2,8192]{2,1,0:T(2,128)(2,1)S(1)} %broadcast_in_dim.94, s32[128]{0:T(128)S(1)} %get-tuple-element.298, bf16[128,2,8192]{2,1,0:T(2,128)(2,1)} %bitcast.7), kind=kCustom, calls=%fused_computation.6 | custom fusion | bytes 12583424 | tf_op jit(solution)/shard_map/scatter | solution.py:97
  247.8 177.5 %all-to-all-done.2 = bf16[32,128,1024]{1,2,0:T(8,128)(2,1)} async-done(((bf16[32,128,1024]{1,2,0:T(8,128)(2,1)}), bf16[32,128,1024]{1,2,0:T(8,128)(2,1)}, u32[]{:S(2)}, u32[]{:S(2)}) %all-to-all-start.2) | async-done | bytes 8388640 | tf_op jit(solution)/shard_map/all_to_all | solution.py:145
  425.4 491.2 %while.18 = (s32[]{:T(128)}, f32[8,8,128]{2,1,0:T(8,128)S(1)}, f32[8,8,128]{2,1,0:T(8,128)S(1)}, f32[8,8,128,128]{3,2,1,0:T(8,128)}, s32[32]{0:T(128)S(1)}, /*in...) while((s32[]{:T(128)}, f32[8,8,128]{2,1,0:T(8,128)S(1)}, ...), condition=%wide.region_13.14_spmd.clone, body=%wide.region_10.13_spmd.clone.sunk | while | flops 551657472 | bytes 25758364 | solution.py:158
  434.9 5.1 fusion.52
  449.4 5.9 fusion.52
  460.4 3.2 fusion.50
  464.8 5.9 fusion.52
  475.8 3.2 fusion.50
  480.2 5.9 fusion.52
  495.6 5.9 fusion.52
  510.9 5.9 fusion.52
  521.9 3.2 fusion.50
  526.3 5.9 fusion.52
  541.7 5.9 fusion.52
  552.7 3.2 fusion.50
  557.1 5.9 fusion.52
  572.4 5.9 fusion.52
  587.8 5.9 fusion.52
  598.8 3.2 fusion.50
  603.2 5.9 fusion.52
  618.6 5.9 fusion.52
  633.9 5.9 fusion.52
  644.9 3.2 fusion.50
  649.3 5.9 fusion.52
  664.7 5.9 fusion.52
  675.7 3.2 fusion.50
  680.0 5.9 fusion.52
  691.0 3.2 fusion.50
  695.4 5.9 fusion.52
  710.8 5.9 fusion.52
  721.8 3.2 fusion.50
  726.2 5.9 fusion.52
  737.1 3.2 fusion.50
  741.5 5.9 fusion.52
  756.9 5.9 fusion.52
  767.9 3.2 fusion.50
  772.3 5.9 fusion.52
  787.7 5.9 fusion.52
  803.0 5.9 fusion.52
  818.4 5.9 fusion.52
  833.8 5.9 fusion.52
  849.1 5.9 fusion.52
  864.5 5.9 fusion.52
  879.9 5.9 fusion.52
  895.3 5.9 fusion.52
  910.6 5.9 fusion.52
  924.6 11.8 %gather_fusion = bf16[128,2,8192]{2,1,0:T(2,128)(2,1)} fusion(bf16[64,2,8192]{2,1,0:T(2,128)(2,1)S(1)} %convert_element_type.46, s32[1024]{0:T(1024)S(1)} %pad_clamp_fusion.1), kind=kCustom, calls=%fused_computation | custom fusion | bytes 8389120 | tf_op jit(solution)/shard_map/gather | solution.py:167
  936.4 6.0 all-to-all-start.5
  942.4 53.2 %all-to-all-done.5 = bf16[128,1,2,8192]{3,2,1,0:T(2,128)(2,1)} async-done(((bf16[128,1,2,8192]{3,2,1,0:T(2,128)(2,1)}), bf16[128,1,2,8192]{3,2,1,0:T(2,128)(2,1)}, u32[]{:S(2)}, u32[]{:S(2)}) %all-to-all-start.5) | async-done | bytes 4194336 | tf_op jit(solution)/shard_map/all_to_all | solution.py:168
  995.6 8.4 gather_fusion.1
  (387 shorter events, 299.7 us)
Async XLA Ops:
  6.5 212.3 %copy-start = (s32[4,2]{0,1:T(2,128)S(1)}, s32[4,2]{0,1:T(2,128)}, u32[]{:S(2)}) copy-start(s32[4,2]{0,1:T(2,128)} %param.13) | copy-start | bytes 100
  6.5 53.8 %copy-start.2 = (bf16[128,1024]{1,0:T(8,128)(2,1)S(1)}, bf16[128,1024]{1,0:T(8,128)(2,1)}, u32[]{:S(2)}) copy-start(bf16[128,1024]{1,0:T(8,128)(2,1)} %param.9) | copy-start | bytes 786436
  9.8 21.5 %all-to-all-start = ((bf16[128,1,1]{2,1,0:T(2,128)(2,1)}), bf16[128,1,1]{2,1,0:T(2,128)(2,1)S(1)}, u32[]{:S(2)}, u32[]{:S(2)}) async-start(bf16[128,1,1]{2,1,0:T(2,128)(2,1)} %copy.45), calls=%async_computation | async-start | bytes 131072 | tf_op jit(solution)/shard_map/all_to_all | solution.py:84
  31.4 23.5 %all-to-all-start.4 = ((bf16[128,1,2,1024]{3,2,1,0:T(2,128)(2,1)}), bf16[128,1,2,1024]{3,2,1,0:T(2,128)(2,1)S(1)}, u32[]{:S(2)}, u32[]{:S(2)}) async-start(bf16[128,1,2,1024]{3,2,1,0:T(2,128)(2,1)} %bitcast.9), calls=%async_computation.4 | async-start | bytes 1048576 | tf_op jit(solution)/shard_map/all_to_all | solution.py:77
  41.1 384.2 %all-gather.2.cloned.1.call-start = ((), (), s32[]{:S(2)}) async-start(), calls=%async_computation.6 | async-start | bytes 8650752 | tf_op jit(solution)/shard_map/all_gather | solution.py:147
  69.4 28.5 %all-to-all-start.1 = ((bf16[128,1,2,1024]{3,2,1,0:T(2,128)(2,1)}), bf16[128,1,2,1024]{3,2,1,0:T(2,128)(2,1)S(1)}, u32[]{:S(2)}, u32[]{:S(2)}) async-start(bf16[128,1,2,1024]{3,2,1,0:T(2,128)(2,1)} %bitcast.4), calls=%async_computation.1 | async-start | bytes 1048576 | tf_op jit(solution)/shard_map/all_to_all | solution.py:70
  97.9 110.9 %all-to-all-start.3 = ((bf16[128,1,2,8192]{3,2,1,0:T(2,128)(2,1)}), bf16[128,1,2,8192]{3,2,1,0:T(2,128)(2,1)}, u32[]{:S(2)}, u32[]{:S(2)}) async-start(bf16[128,1,2,8192]{3,2,1,0:T(2,128)(2,1)} %bitcast.79), calls=%async_computation.3 | async-start | bytes 8388608 | tf_op jit(solution)/shard_map/all_to_all | solution.py:63
  213.9 211.5 %all-to-all-start.2 = ((bf16[32,128,1024]{1,2,0:T(8,128)(2,1)}), bf16[32,128,1024]{1,2,0:T(8,128)(2,1)}, u32[]{:S(2)}, u32[]{:S(2)}) async-start(bf16[32,128,1024]{1,2,0:T(8,128)(2,1)} %stack.3), calls=%async_computation.2 | async-start | bytes 16777216 | tf_op jit(solution)/shard_map/all_to_all | solution.py:145
  936.4 59.2 %all-to-all-start.5 = ((bf16[128,1,2,8192]{3,2,1,0:T(2,128)(2,1)}), bf16[128,1,2,8192]{3,2,1,0:T(2,128)(2,1)}, u32[]{:S(2)}, u32[]{:S(2)}) async-start(bf16[128,1,2,8192]{3,2,1,0:T(2,128)(2,1)} %bitcast.80), calls=%async_computation.5 | async-start | bytes 8388608 | tf_op jit(solution)/shard_map/all_to_all | solution.py:168
  995.6 10.6 %copy-start.1 = (s32[4,2]{0,1:T(2,128)S(1)}, s32[4,2]{0,1:T(2,128)}, u32[]{:S(2)}) copy-start(s32[4,2]{0,1:T(2,128)} %param.13) | copy-start | bytes 100
Sparse Core Ops, SparseCore 0:
  60.4 337.4 all-gather.1
